TPU v7x, 512 devices: a whole 4x8x8 slice. The times are simulated.
512 devices in a mesh: row: 64 (over z_lo, y, core), rep: 8 (over x, z_hi).
Axes of the slice: x: 4, y: 8, z: 8 (z_hi: 2, z_lo: 4; z = z_hi * 4 + z_lo), core: 2. Of those that a mesh axis runs over, the one named last changes fastest.
Arguments:
- features: float32 [131072, 256], P(('row', 'rep')), may hold values from -6 to 6
- weight: float32 [256, 256], replicated, may hold values from -0.375 to 0.375
- cotangent: float32 [131072, 256], P(('row', 'rep')), may hold values from -6 to 6
- tile_values: float32 [64, 8, 40, 128, 128], P('row', 'rep'), may hold values from -0.125 to 0.125
- tile_pos: int32 [64, 8, 40], P('row', 'rep'), may hold values from 0 to 127, as said below
- tile_count: int32 [64, 8], P('row', 'rep'), may hold values from 5 to 40, as said below
Outputs:
- activation: float32 [131072, 256], P(('row', 'rep'))
- grad_features: float32 [131072, 256], P(('row', 'rep'))
- grad_weight: float32 [256, 256], replicated
Inputs may be any that keep to these rules, and one draw needn't show every extreme that they name: `tile_pos`: the 40 slots of one device hold distinct positions. `tile_count`: some device has all 40 slots live.
All inputs are finite; a program needn't handle non-finite values.
Results may differ from a plain program's by a relative error of at most 0.0003.
Values sent between devices are 32-bit elements; how exact they have to be, the bound alone decides.
A program may use at most 64 MiB of HBM per device.

v0:
```python
import math

import jax
import jax.numpy as jnp
from jax import lax
from jax.sharding import PartitionSpec as P

HID = 256
TILE = 128
STOPS = 4


def passed_along(block, axis, distance):
    devices = range(lax.axis_size(axis))
    route = [((i - distance) % len(devices), i) for i in devices]
    return lax.ppermute(block, axis, route)


def body(features, weight, cotangent, tile_values, tile_pos, tile_count):
    share_rows = features.shape[0]
    groups = lax.axis_size("rep")
    share_blocks = share_rows // TILE
    tile_rows = share_blocks * groups
    positions = STOPS * share_blocks
    values_here = tile_values[0, 0]
    pos_here = tile_pos[0, 0]
    count_here = tile_count[0, 0]
    pieces = [features]
    current = features
    for stop in range(1, STOPS):
        current = passed_along(current, "row", 1)
        pieces.append(current)
    band = jnp.stack(pieces, axis=0).reshape(positions, TILE, HID)
    source = pos_here % positions
    target = pos_here // positions
    live_slots = (jnp.arange(values_here.shape[0]) < count_here).astype(jnp.float32)
    picked = jnp.take(band, source, axis=0)
    product = jnp.einsum("kij,kjh->kih", values_here, picked, precision=lax.Precision.HIGHEST)
    onehot = (target[None, :] == jnp.arange(tile_rows)[:, None]).astype(jnp.float32) * live_slots[
        None, :
    ]
    summed = jnp.einsum("tk,kih->tih", onehot, product, precision=lax.Precision.HIGHEST)
    mine = lax.psum_scatter(
        summed.reshape(lax.axis_size("rep") * share_rows, HID),
        "rep",
        scatter_dimension=0,
        tiled=True,
    )
    preact = jnp.dot(
        mine, weight, precision=lax.Precision.HIGHEST, preferred_element_type=jnp.float32
    )
    squashed = jax.nn.sigmoid(preact)
    activation = preact * squashed
    slopes = cotangent * squashed * (1.0 + preact * (1.0 - squashed))
    local_weight = jnp.dot(
        mine.T, slopes, precision=lax.Precision.HIGHEST, preferred_element_type=jnp.float32
    )
    node_total = share_rows * lax.axis_size("row") * groups
    grad_weight = lax.psum(local_weight, ("row", "rep")) / math.sqrt(node_total)
    back_share = jnp.dot(
        slopes, weight.T, precision=lax.Precision.HIGHEST, preferred_element_type=jnp.float32
    )
    rows_grad = lax.all_gather(back_share, "rep", axis=0, tiled=True).reshape(tile_rows, TILE, HID)
    picked_back = jnp.take(rows_grad, target, axis=0)
    contrib = jnp.einsum("kji,kjh->kih", values_here, picked_back, precision=lax.Precision.HIGHEST)
    onehot_back = (source[None, :] == jnp.arange(positions)[:, None]).astype(
        jnp.float32
    ) * live_slots[None, :]
    spread = jnp.einsum("qk,kih->qih", onehot_back, contrib, precision=lax.Precision.HIGHEST)
    spread = spread.reshape(STOPS, share_rows, HID)
    running = spread[STOPS - 1]
    for stop in range(STOPS - 2, -1, -1):
        running = passed_along(running, "row", -1) + spread[stop]
    return (activation, running, grad_weight)


def solution(mesh):
    in_specs = (
        P(("row", "rep"), None),
        P(),
        P(("row", "rep"), None),
        P("row", "rep", None, None, None),
        P("row", "rep", None),
        P("row", "rep"),
    )
    out_specs = (P(("row", "rep"), None), P(("row", "rep"), None), P())
    return jax.shard_map(body, mesh=mesh, in_specs=in_specs, out_specs=out_specs, check_vma=False)
```

profile of v0, /device:TPU:1, one launch (start us, length us, event | category | flops | bytes accessed | tf_op | source)
XLA Modules:
  0.0 571.1 jit_solution(5161946536979627714)
XLA Ops:
  7.2 0.0 copy-start
  7.2 0.0 reduce-scatter.2.cloned.1.call-start
  7.2 4.7 collective-permute-start
  12.0 5.4 collective-permute-done
  17.4 2.5 collective-permute-start.1
  19.9 0.7 fusion.26
  20.5 8.4 %collective-permute-done.1 = f32[256,256]{1,0:T(8,128)S(1)} collective-permute-done((f32[256,256]{1,0:T(8,128)S(1)}, f32[256,256]{1,0:T(8,128)S(1)}, u32[]{:S(2)}, u32[]{:S(2)}) %collective-permute-start.1) | collective-permute-done | bytes 262176 | tf_op jit(solution)/shard_map/ppermute | solution.py:16
  29.0 1.9 collective-permute-start.2
  31.5 0.7 compare_and_fusion
  32.2 8.3 %collective-permute-done.2 = f32[256,256]{1,0:T(8,128)S(1)} collective-permute-done((f32[256,256]{1,0:T(8,128)S(1)}, f32[256,256]{1,0:T(8,128)S(1)}, u32[]{:S(2)}, u32[]{:S(2)}) %collective-permute-start.2) | collective-permute-done | bytes 262176 | tf_op jit(solution)/shard_map/ppermute | solution.py:16
  40.6 2.0 pad_maximum_fusion
  42.6 4.4 gather_fusion
  47.0 0.0 copy-done
  47.0 12.7 %fusion.6 = f32[40,256,128]{2,1,0:T(8,128)} fusion(f32[40,128,256]{2,1,0:T(8,128)} %gather_fusion, f32[1,1,40,128,128]{4,3,2,1,0:T(8,128)S(1)} %copy-done, pred[40]{0:T(512)(128)(4,1)S(1)} %get-tuple-element.13), kind=kOutput, calls=%fused_computation.8 | convolution fusion | flops 2014576640 | bytes 13107240 | tf_op jit(solution)/shard_map/kij,kjh->kih/dot_general | solution.py:38
  59.7 6.2 %copy.14 = f32[40,256,128]{1,0,2:T(8,128)} copy(f32[40,256,128]{2,1,0:T(8,128)} %fusion.6) | data formatting | bytes 10485760 | tf_op jit(solution)/shard_map/kij,kjh->kih/dot_general | solution.py:38
  65.9 0.0 copy-start.1
  65.9 4.7 fusion.2
  70.6 0.0 copy-start.2
  70.6 2.6 copy.9
  73.2 0.0 reduce-scatter.2.cloned.1.call-update
  73.2 0.0 all-gather.2.cloned.1.call-start
  73.2 101.5 %reduce-scatter.2.cloned.1.call-done = f32[256,256]{1,0:T(8,128)} async-done(((f32[2048,256]{1,0:T(8,128)}), f32[256,256]{1,0:T(8,128)}) %reduce-scatter.2.cloned.1.call-update) | async-done | bytes 262160 | tf_op jit(solution)/shard_map/reduce_scatter | solution.py:43
  174.7 0.0 copy-done.1
  174.8 2.1 fusion.14
  176.8 0.0 copy-start.5
  176.8 0.7 copy-done.5
  177.5 0.0 copy-done.2
  177.5 1.2 fusion.32
  178.7 0.0 all-gather.2.cloned.1.call-update
  178.7 0.2 all-reduce.2.cloned.1.call-start
  178.9 77.8 %all-gather.2.cloned.1.call-done = f32[2048,256]{1,0:T(8,128)} async-done(((f32[256,256]{1,0:T(8,128)}), f32[2048,256]{1,0:T(8,128)}) %all-gather.2.cloned.1.call-update) | async-done | bytes 2097168 | tf_op jit(solution)/shard_map/all_gather | solution.py:63
  256.8 4.8 gather_fusion.1
  261.6 12.7 %fusion.4 = f32[40,256,128]{2,1,0:T(8,128)} fusion(f32[40,128,256]{2,1,0:T(8,128)} %gather_fusion.1, f32[1,1,40,128,128]{4,3,2,1,0:T(8,128)S(1)} %copy-done, pred[40]{0:T(512)(128)(4,1)S(1)} %get-tuple-element.3), kind=kOutput, calls=%fused_computation.6 | convolution fusion | flops 2014576640 | bytes 13107240 | tf_op jit(solution)/shard_map/kji,kjh->kih/dot_general | solution.py:65
  274.3 6.2 %copy.15 = f32[40,256,128]{1,0,2:T(8,128)} copy(f32[40,256,128]{2,1,0:T(8,128)} %fusion.4) | data formatting | bytes 10485760 | tf_op jit(solution)/shard_map/kji,kjh->kih/dot_general | solution.py:65
  280.5 0.0 copy-start.3
  280.5 0.0 copy-start.4
  280.5 0.0 copy-start.6
  280.5 4.6 fusion
  285.0 0.4 fusion.33
  285.4 3.9 collective-permute-start.3
  289.3 5.1 collective-permute-done.3
  294.5 2.6 collective-permute-start.4
  297.1 0.0 copy-done.3
  297.1 0.0 copy-done.4
  297.1 0.0 copy-done.6
  297.1 1.3 fusion.31
  298.4 0.0 all-reduce.2.cloned.1.call-update
  298.5 3.8 collective-permute-done.4
  302.3 1.0 bitcast_add_fusion.1
  303.2 6.4 %collective-permute-start.5 = (f32[256,256]{1,0:T(8,128)S(1)}, f32[256,256]{1,0:T(8,128)S(1)}, u32[]{:S(2)}, u32[]{:S(2)}) collective-permute-start(f32[256,256]{1,0:T(8,128)S(1)} %bitcast_add_fusion.1), channel_id=1, source_target_pairs={{8,0},{16,8},{24,16},{32,24},{40,32},{48,40},{56,48},{64,56},{72,6... | collective-permute-start | bytes 786440 | tf_op jit(solution)/shard_map/ppermute | solution.py:16
  309.6 252.5 %all-reduce.2.cloned.1.call-done = f32[256,256]{1,0:T(8,128)} async-done(((f32[256,256]{1,0:T(8,128)}), f32[256,256]{1,0:T(8,128)}) %all-reduce.2.cloned.1.call-update) | async-done | bytes 262160 | tf_op jit(solution)/shard_map/psum | solution.py:59
  562.1 1.7 broadcast_multiply_fusion
  563.8 0.0 collective-permute-done.5
  563.8 0.7 bitcast_add_fusion
  (7 shorter events, 0.1 us)
Async XLA Ops:
  7.2 39.9 %copy-start = (f32[1,1,40,128,128]{4,3,2,1,0:T(8,128)S(1)}, f32[1,1,40,128,128]{4,3,2,1,0:T(8,128)}, u32[]{:S(2)}) copy-start(f32[1,1,40,128,128]{4,3,2,1,0:T(8,128)} %param.9) | copy-start | bytes 7864324
  7.2 167.6 %reduce-scatter.2.cloned.1.call-start = ((), (), s32[]{:S(2)}) async-start(), calls=%async_computation.1 | async-start | bytes 2359296 | tf_op jit(solution)/shard_map/reduce_scatter | solution.py:43
  7.2 10.2 %collective-permute-start = (f32[256,256]{1,0:T(8,128)}, f32[256,256]{1,0:T(8,128)S(1)}, u32[]{:S(2)}, u32[]{:S(2)}) collective-permute-start(f32[256,256]{1,0:T(8,128)} %param.6), channel_id=1, source_target_pairs={{504,0},{0,8},{8,16},{16,24},{24,32},{32,40},{40,48},{48,56},{56,6... | collective-permute-start | bytes 786440 | tf_op jit(solution)/shard_map/ppermute | solution.py:16
  17.4 11.6 %collective-permute-start.1 = (f32[256,256]{1,0:T(8,128)S(1)}, f32[256,256]{1,0:T(8,128)S(1)}, u32[]{:S(2)}, u32[]{:S(2)}) collective-permute-start(f32[256,256]{1,0:T(8,128)S(1)} %collective-permute-done), channel_id=1, source_target_pairs={{504,0},{0,8},{8,16},{16,24},{24,32},{32,40},{40,48},{48,56},{56,6... | collective-permute-start | bytes 786440 | tf_op jit(solution)/shard_map/ppermute | solution.py:16
  29.0 11.6 %collective-permute-start.2 = (f32[256,256]{1,0:T(8,128)S(1)}, f32[256,256]{1,0:T(8,128)S(1)}, u32[]{:S(2)}, u32[]{:S(2)}) collective-permute-start(f32[256,256]{1,0:T(8,128)S(1)} %collective-permute-done.1), channel_id=1, source_target_pairs={{504,0},{0,8},{8,16},{16,24},{24,32},{32,40},{40,48},{48,56},{56,6... | collective-permute-start | bytes 786440 | tf_op jit(solution)/shard_map/ppermute | solution.py:16
  65.9 108.8 %copy-start.1 = (f32[256,256]{1,0:T(8,128)S(1)}, f32[256,256]{1,0:T(8,128)}, u32[]{:S(2)}) copy-start(f32[256,256]{1,0:T(8,128)} %param.7) | copy-start | bytes 786436
  70.6 106.9 %copy-start.2 = (f32[256,256]{1,0:T(8,128)S(1)}, f32[256,256]{1,0:T(8,128)}, u32[]{:S(2)}) copy-start(f32[256,256]{1,0:T(8,128)} %param.8) | copy-start | bytes 786436
  73.2 183.6 %all-gather.2.cloned.1.call-start = ((), (), s32[]{:S(2)}) async-start(), calls=%async_computation.2 | async-start | bytes 2359296 | tf_op jit(solution)/shard_map/all_gather | solution.py:63
  176.8 0.7 copy-start.5
  178.7 383.4 %all-reduce.2.cloned.1.call-start = ((), (), s32[]{:S(2)}) async-start(), calls=%async_computation.3 | async-start | bytes 524288 | tf_op jit(solution)/shard_map/psum | solution.py:59
  280.5 16.6 %copy-start.3 = (f32[256,256]{1,0:T(8,128)S(1)}, f32[256,256]{1,0:T(8,128)}, u32[]{:S(2)}) copy-start(f32[256,256]{1,0:T(8,128)} %param.8) | copy-start | bytes 786436
  280.5 16.6 %copy-start.4 = (f32[256,256]{1,0:T(8,128)S(1)}, f32[256,256]{1,0:T(8,128)}, u32[]{:S(2)}) copy-start(f32[256,256]{1,0:T(8,128)} %reduce-scatter.2.cloned.1.call-done) | copy-start | bytes 786436
  280.5 16.6 %copy-start.6 = (f32[256,256]{1,0:T(8,128)S(1)}, f32[256,256]{1,0:T(8,128)}, u32[]{:S(2)}) copy-start(f32[256,256]{1,0:T(8,128)} %copy-done.5) | copy-start | bytes 786436
  285.4 9.0 %collective-permute-start.3 = (f32[256,256]{1,0:T(8,128)S(1)}, f32[256,256]{1,0:T(8,128)S(1)}, u32[]{:S(2)}, u32[]{:S(2)}) collective-permute-start(f32[256,256]{1,0:T(8,128)S(1)} %bitcast.78), channel_id=1, source_target_pairs={{8,0},{16,8},{24,16},{32,24},{40,32},{48,40},{56,48},{64,56},{72,6... | collective-permute-start | bytes 786440 | tf_op jit(solution)/shard_map/ppermute | solution.py:16
  294.5 7.8 %collective-permute-start.4 = (f32[256,256]{1,0:T(8,128)S(1)}, f32[256,256]{1,0:T(8,128)}, u32[]{:S(2)}, u32[]{:S(2)}) collective-permute-start(f32[256,256]{1,0:T(8,128)S(1)} %bitcast_add_fusion.2), channel_id=1, source_target_pairs={{8,0},{16,8},{24,16},{32,24},{40,32},{48,40},{56,48},{64,56},{72,6... | collective-permute-start | bytes 786440 | tf_op jit(solution)/shard_map/ppermute | solution.py:16
  303.2 260.6 %collective-permute-start.5 = (f32[256,256]{1,0:T(8,128)S(1)}, f32[256,256]{1,0:T(8,128)S(1)}, u32[]{:S(2)}, u32[]{:S(2)}) collective-permute-start(f32[256,256]{1,0:T(8,128)S(1)} %bitcast_add_fusion.1), channel_id=1, source_target_pairs={{8,0},{16,8},{24,16},{32,24},{40,32},{48,40},{56,48},{64,56},{72,6... | collective-permute-start | bytes 786440 | tf_op jit(solution)/shard_map/ppermute | solution.py:16
Sparse Core Ops, SparseCore 0:
  73.3 101.3 reduce-scatter.1
  179.0 77.7 all-gather.1
  298.5 263.5 all-reduce.1
where the time goes:
time: 572 us; the launch traced here: 571 us
  waiting for transfers between devices  463 us (81%)
  matrix products  39.2 us (7%)
  local copies, waits for them, and re-layouts  25.3 us (4%)
  starting transfers between devices  22.2 us (4%)
  between operations  14.6 us (3%)
  other arithmetic  6.82 us (1%)
    psum x1, waiting for transfers between devices, body(): grad_weight = lax.psum(local_weight, ('row', 'rep')) / math.sqrt(node_total)  253 us
    reduce_scatter x1, waiting for transfers between devices, body(): lax.psum_scatter(summed.reshape(lax.axis_size('rep') * share_rows, HID),...  102 us
    all_gather x1, waiting for transfers between devices, body(): lax.all_gather(back_share, 'rep', axis=0, tiled=True)  77.8 us
    ppermute x6, waiting for transfers between devices, passed_along(): return lax.ppermute(block, axis, route)  31.1 us
    ppermute x6, starting transfers between devices, passed_along(): return lax.ppermute(block, axis, route)  21.9 us
    dot_general x1, matrix products, body(): jnp.einsum('kij,kjh->kih', values_here, picked, precision=lax.Precision.H...  12.7 us
    dot_general x1, matrix products, body(): jnp.einsum('kji,kjh->kih', values_here, picked_back, precision=lax.Precis...  12.7 us
  transfers between devices with their start and end apart: 9, of which 8 were waited for; matrix products, arithmetic and copies ran while one was open for 1% of the time, Pallas kernels for 0%

commit v1 on v0

v1 whole, which is shorter than its diff:
```python
import functools
import math

import jax
import jax.numpy as jnp
from jax import lax
from jax.experimental import pallas as pl
from jax.experimental.pallas import tpu as pltpu
from jax.sharding import PartitionSpec as P

HID = 256
TILE = 128
STOPS = 4
KMAX = 40
ROWS = 256
HALF = 128
NX = 4
NY = 8
NZ = 8
SLABS = 64
MESH = pl.DeviceIdType.MESH
BF = jnp.bfloat16
F32 = jnp.float32


def split(value):
    high = value.astype(BF)
    low = (value - high.astype(F32)).astype(BF)
    return high, low


def dot(a, b, contract=((1,), (0,))):
    return lax.dot_general(a, b, (contract, ((), ())), preferred_element_type=F32)


def dot3(a, b, contract=((1,), (0,))):
    a_hi, a_lo = a
    b_hi, b_lo = b
    return dot(a_hi, b_hi, contract) + (dot(a_hi, b_lo, contract) + dot(a_lo, b_hi, contract))


def kernel(
    inv, feat, weight, cot, tiles_hbm, act, gf, gw,
    tiles, a_hi, a_lo, t_hi, t_lo, band, x_cat, pbuf, rx1, rx2, zsend, zrecv, mine,
    g, sp, rr, lw, cr, yr, xr, zz, wh, gwb,
    load_sem, band_s, band_r, rs_s, rs_r, zx_s, zx_r, ag_s, ag_r, az_s, az_r, ring_s, ring_r,
    red_s, red_r,
):
    row = lax.axis_index("row")
    rep = lax.axis_index("rep")
    core = lax.rem(row, 2)
    y = lax.rem(row // 2, NY)
    z_lo = row // 16
    x = rep // 2
    z_hi = lax.rem(rep, 2)
    z = z_hi * 4 + z_lo

    def device(core_, y_, z_, x_):
        return (lax.rem(z_, 4) * 16 + y_ * 2 + core_, x_ * 2 + z_ // 4)

    x_right = lax.rem(x + 1, NX)
    x_opp = lax.rem(x + 2, NX)
    x_left = lax.rem(x + 3, NX)
    right = (row, x_right * 2 + z_hi)
    left = (row, x_left * 2 + z_hi)
    across = (row, x * 2 + 1 - z_hi)
    partner = (row + 1 - 2 * core, rep)
    following = (lax.rem(row + 1, SLABS), rep)
    previous = (lax.rem(row + SLABS - 1, SLABS), rep)
    y_peers = [device(core, lax.rem(y + k, NY), z, x) for k in range(1, NY)]
    x_peers = [device(core, y, z, lax.rem(x + k, NX)) for k in range(1, NX)]
    z_peers = [device(core, y, lax.rem(z + k, NZ), x) for k in range(1, NZ)]

    started = []

    def send(src, dst, s_sem, r_sem, to):
        copy = pltpu.make_async_remote_copy(
            src_ref=src, dst_ref=dst, send_sem=s_sem, recv_sem=r_sem,
            device_id=to, device_id_type=MESH,
        )
        copy.start()
        started.append(copy)
        return copy

    loads = [
        pltpu.make_async_copy(feat.at[:, pl.ds(c * HALF, HALF)], band.at[0, c], load_sem.at[c])
        for c in range(2)
    ]
    loads.append(pltpu.make_async_copy(tiles_hbm, tiles.at[pl.ds(0, KMAX)], load_sem.at[2]))
    for copy in loads:
        copy.start()

    barrier = pltpu.get_barrier_semaphore()
    greeted = [following, previous, partner] + y_peers + x_peers + z_peers
    for peer in greeted:
        pl.semaphore_signal(barrier, inc=1, device_id=peer, device_id_type=MESH)
    tiles[KMAX] = jnp.zeros((TILE, TILE), F32)
    loads[0].wait()
    loads[1].wait()
    pl.semaphore_wait(barrier, len(greeted))

    band_copy = {}

    def band_send(s, c):
        band_copy[s, c] = send(
            band.at[s, c], band.at[s + 1, c], band_s.at[s, c], band_r.at[s, c], following
        )

    def band_take(s, c):
        high, low = split(band[s, c])
        x_cat[c, s * ROWS:(s + 1) * ROWS, 0:HALF] = high
        x_cat[c, s * ROWS:(s + 1) * ROWS, HALF:2 * HALF] = low

    def band_step(s, c):
        band_copy[s, c].wait_recv()
        if s + 1 < STOPS - 1:
            band_send(s + 1, c)
        band_take(s + 1, c)

    band_send(0, 0)
    band_send(0, 1)
    band_take(0, 0)
    band_take(0, 1)
    loads[2].wait()

    def fill_rows(d, carry):
        for half in range(2):
            for q in range(8):
                tile = tiles[inv[(d * 2 + half) * 8 + q]]
                high, low = split(tile)
                a_hi[d, half * TILE:(half + 1) * TILE, q * TILE:(q + 1) * TILE] = high
                a_lo[d, half * TILE:(half + 1) * TILE, q * TILE:(q + 1) * TILE] = low
        return carry

    def fill_turned(i, carry):
        xq = i // STOPS
        s = lax.rem(i, STOPS)
        for tt in range(4):
            for j in range(2):
                tile = tiles[inv[(xq * 4 + tt) * 8 + s * 2 + j]]
                high, low = split(tile.T)
                t_hi[xq, s, j * TILE:(j + 1) * TILE, tt * TILE:(tt + 1) * TILE] = high
                t_lo[xq, s, j * TILE:(j + 1) * TILE, tt * TILE:(tt + 1) * TILE] = low
        return carry

    def turn(part):
        lax.fori_loop(part * 4, part * 4 + 4, fill_turned, 0)

    lax.fori_loop(0, 2, fill_rows, 0)
    band_step(0, 0)
    lax.fori_loop(2, 4, fill_rows, 0)
    band_step(0, 1)
    lax.fori_loop(4, 6, fill_rows, 0)
    band_step(1, 0)
    lax.fori_loop(6, 8, fill_rows, 0)
    band_step(1, 1)
    band_step(2, 0)

    units = [(0, 0), (0, 1), (1, 0), (1, 1)]
    rs_copy = {}

    def partial_rows(u, place, x_to):
        own, c = units[u]
        d = x_to * 2 + (z_hi if own else 1 - z_hi)
        both = dot(a_hi[d], x_cat[c])
        rest = dot(a_lo[d], x_cat[c, :, 0:HALF])
        pbuf[u, place] = both[:, 0:HALF] + (both[:, HALF:2 * HALF] + rest)

    upper = pl.ds(0, HALF)
    lower = pl.ds(HALF, HALF)

    def rs_send(u, k, src, dst, to):
        rs_copy[u, k] = send(src, dst, rs_s.at[u, k], rs_r.at[u, k], to)

    def rs_begin(u):
        partial_rows(u, 0, x_opp)
        rs_send(u, 0, pbuf.at[u, 0, upper], rx1.at[u, 0], right)
        rs_send(u, 1, pbuf.at[u, 0, lower], rx1.at[u, 1], left)
        partial_rows(u, 1, x_right)
        rs_send(u, 2, pbuf.at[u, 1, lower], rx2.at[u, 0, lower], right)
        partial_rows(u, 2, x_left)
        rs_send(u, 3, pbuf.at[u, 2, upper], rx2.at[u, 1, upper], left)
        partial_rows(u, 3, x)

    def rs_relay(u):
        rs_copy[u, 0].wait_recv()
        pbuf[u, 1, upper] = pbuf[u, 1, upper] + rx1[u, 0]
        rs_send(u, 4, pbuf.at[u, 1, upper], rx2.at[u, 0, upper], right)
        rs_copy[u, 1].wait_recv()
        pbuf[u, 2, lower] = pbuf[u, 2, lower] + rx1[u, 1]
        rs_send(u, 5, pbuf.at[u, 2, lower], rx2.at[u, 1, lower], left)

    zx_copy = {}

    def rs_finish(u):
        own, c = units[u]
        for k in (2, 3, 4, 5):
            rs_copy[u, k].wait_recv()
        total = pbuf[u, 3] + (rx2[u, 0] + rx2[u, 1])
        if own:
            zx_copy[c].wait_recv()
            mine[:, c * HALF:(c + 1) * HALF] = total + zrecv[c]
        else:
            zsend[c] = total
            zx_copy[c] = send(zsend.at[c], zrecv.at[c], zx_s.at[c], zx_r.at[c], across)

    rs_begin(0)
    band_step(2, 1)
    rs_begin(1)
    rs_relay(0)
    turn(0)
    rs_begin(2)
    rs_relay(1)
    rs_finish(0)
    turn(1)
    rs_begin(3)
    rs_relay(2)
    rs_finish(1)
    turn(2)
    rs_relay(3)
    turn(3)
    w_parts = split(weight[...])
    rs_finish(2)
    rs_finish(3)

    total = mine[...]
    preact = dot3(split(total), w_parts)
    squashed = jax.nn.sigmoid(preact)
    act[...] = preact * squashed
    slopes = cot[...] * squashed * (1.0 + preact * (1.0 - squashed))
    s_parts = split(slopes)

    ag_copy = {}
    az_copy = {}

    def ag_send(own, c, k, src, to):
        ag_copy[own, c, k] = send(src, src, ag_s.at[own, c, k], ag_r.at[own, c, k], to)

    for c in range(2):
        w_rows = (w_parts[0][c * HALF:(c + 1) * HALF, :], w_parts[1][c * HALF:(c + 1) * HALF, :])
        g[rep, c] = dot3(s_parts, w_rows, ((1,), (1,)))
        block = g.at[rep, c]
        az_copy[c] = send(block, block, az_s.at[c], az_r.at[c], across)
        ag_send(1, c, 0, block, right)
        ag_send(1, c, 1, block, left)

    red_copy = {}

    def red_send(k, src, dst, to):
        red_copy[k] = send(src, dst, red_s.at[k], red_r.at[k], to)

    turned = split(total.T)
    for c in range(2):
        lw[c] = dot3(turned, (s_parts[0][:, c * HALF:(c + 1) * HALF], s_parts[1][:, c * HALF:(c + 1) * HALF]))
    red_send(0, lw.at[1 - core], cr, partner)

    def red_y():
        red_copy[0].wait_recv()
        lw[core] = lw[core] + cr[...]
        for k in range(1, NY):
            rows = pl.ds(pl.multiple_of(lax.rem(y + k, NY) * 32, 32), 32)
            red_send(k, lw.at[core, rows], yr.at[y], y_peers[k - 1])
        yr[y] = lw[core, pl.ds(pl.multiple_of(y * 32, 32), 32)]

    def red_x():
        for k in range(1, NY):
            red_copy[k].wait_recv()
        yr[0] = jnp.sum(yr[...], axis=0)
        for k in range(1, NX):
            rows = pl.ds(pl.multiple_of(lax.rem(x + k, NX) * 8, 8), 8)
            red_send(7 + k, yr.at[0, rows], xr.at[x], x_peers[k - 1])
        xr[x] = yr[0, pl.ds(pl.multiple_of(x * 8, 8), 8)]

    def red_z():
        for k in range(1, NX):
            red_copy[7 + k].wait_recv()
        zz[z] = jnp.sum(xr[...], axis=0)
        for k in range(1, NZ):
            red_send(10 + k, zz.at[z], zz.at[z], z_peers[k - 1])

    def red_x_back():
        for k in range(1, NZ):
            red_copy[10 + k].wait_recv()
        rows = pl.ds(pl.multiple_of(y * 32 + x * 8, 8), 8)
        wh[rows] = jnp.sum(zz[...], axis=0) * (1.0 / math.sqrt(SLABS * 8 * ROWS))
        for k in range(1, NX):
            red_send(17 + k, wh.at[rows], wh.at[rows], x_peers[k - 1])

    def red_y_back():
        for k in range(1, NX):
            red_copy[17 + k].wait_recv()
        rows = pl.ds(pl.multiple_of(y * 32, 32), 32)
        for k in range(1, NY):
            red_send(20 + k, wh.at[rows], wh.at[rows], y_peers[k - 1])

    def red_core_back():
        for k in range(1, NY):
            red_copy[20 + k].wait_recv()
        gwb[core] = wh[...]
        red_send(28, gwb.at[core], gwb.at[core], partner)

    def ag_relay(own, c):
        w = z_hi if own else 1 - z_hi
        ag_copy[own, c, 0].wait_recv()
        ag_send(own, c, 2, g.at[x_left * 2 + w, c, upper], right)
        ag_copy[own, c, 1].wait_recv()
        ag_send(own, c, 3, g.at[x_right * 2 + w, c, lower], left)

    def ag_across(c):
        az_copy[c].wait_recv()
        block = g.at[x * 2 + 1 - z_hi, c]
        ag_send(0, c, 0, block, right)
        ag_send(0, c, 1, block, left)

    def ag_last(c):
        for own in range(2):
            for k in (2, 3):
                ag_copy[own, c, k].wait_recv()

    def spread(xq, c, first=False):
        for j in range(2):
            high, low = split(g[xq * 2 + j, c])
            x_cat[c, j * ROWS:(j + 1) * ROWS, 0:HALF] = high
            x_cat[c, j * ROWS:(j + 1) * ROWS, HALF:2 * HALF] = low

        def one_stop(s, carry):
            both = dot(t_hi[xq, s], x_cat[c, 0:2 * ROWS])
            rest = dot(t_lo[xq, s], x_cat[c, 0:2 * ROWS, 0:HALF])
            term = both[:, 0:HALF] + (both[:, HALF:2 * HALF] + rest)
            sp[c, s] = term if first else sp[c, s] + term
            return carry

        lax.fori_loop(0, STOPS, one_stop, 0)

    ring_copy = {}

    def ring_send(c, step):
        ring_copy[c, step] = send(
            sp.at[c, STOPS - 1 - step], rr.at[step, c], ring_s.at[c, step], ring_r.at[c, step],
            previous,
        )

    def ring_step(c, step):
        ring_copy[c, step].wait_recv()
        s = STOPS - 2 - step
        if s > 0:
            sp[c, s] = sp[c, s] + rr[step, c]
            ring_send(c, step + 1)
        else:
            gf[:, c * HALF:(c + 1) * HALF] = sp[c, 0] + rr[step, c]

    ag_relay(1, 0)
    ag_across(0)
    red_y()
    ag_relay(1, 1)
    ag_across(1)
    spread(x, 0, first=True)
    spread(x, 1, first=True)
    red_x()
    ag_relay(0, 0)
    spread(x_right, 0)
    spread(x_left, 0)
    red_z()
    ag_relay(0, 1)
    spread(x_right, 1)
    spread(x_left, 1)
    red_x_back()
    ag_last(0)
    spread(x_opp, 0)
    ring_send(0, 0)
    red_y_back()
    ag_last(1)
    spread(x_opp, 1)
    ring_send(1, 0)
    ring_step(0, 0)
    red_core_back()
    ring_step(1, 0)
    ring_step(0, 1)
    ring_step(1, 1)
    ring_step(0, 2)
    ring_step(1, 2)
    red_copy[28].wait_recv()
    gw[:, 0:HALF] = gwb[0]
    gw[:, HALF:2 * HALF] = gwb[1]
    for copy in started:
        copy.wait_send()


def layer(inv, features, weight, cotangent, tiles):
    vmem = pl.BlockSpec(memory_space=pltpu.VMEM)
    hbm = pl.BlockSpec(memory_space=pl.ANY)
    dma = lambda *shape: pltpu.SemaphoreType.DMA(shape)
    block = (ROWS, HALF)
    scratch = [
        pltpu.VMEM((KMAX + 1, TILE, TILE), F32),
        pltpu.VMEM((8, ROWS, STOPS * ROWS), BF),
        pltpu.VMEM((8, ROWS, STOPS * ROWS), BF),
        pltpu.VMEM((NX, STOPS, ROWS, 2 * ROWS), BF),
        pltpu.VMEM((NX, STOPS, ROWS, 2 * ROWS), BF),
        pltpu.VMEM((STOPS, 2) + block, F32),
        pltpu.VMEM((2, STOPS * ROWS, 2 * HALF), BF),
        pltpu.VMEM((4, 4) + block, F32),
        pltpu.VMEM((4, 2, HALF, HALF), F32),
        pltpu.VMEM((4, 2) + block, F32),
        pltpu.VMEM((2,) + block, F32),
        pltpu.VMEM((2,) + block, F32),
        pltpu.VMEM((ROWS, HID), F32),
        pltpu.VMEM((8, 2) + block, F32),
        pltpu.VMEM((2, STOPS) + block, F32),
        pltpu.VMEM((STOPS - 1, 2) + block, F32),
        pltpu.VMEM((2,) + block, F32),
        pltpu.VMEM(block, F32),
        pltpu.VMEM((NY, 32, HALF), F32),
        pltpu.VMEM((NX, 8, HALF), F32),
        pltpu.VMEM((NZ, 8, HALF), F32),
        pltpu.VMEM(block, F32),
        pltpu.VMEM((2,) + block, F32),
        dma(3),
        dma(3, 2), dma(3, 2),
        dma(4, 6), dma(4, 6),
        dma(2), dma(2),
        dma(2, 2, 4), dma(2, 2, 4),
        dma(2), dma(2),
        dma(2, 3), dma(2, 3),
        dma(29), dma(29),
    ]
    return pl.pallas_call(
        kernel,
        out_shape=(
            jax.ShapeDtypeStruct((ROWS, HID), F32),
            jax.ShapeDtypeStruct((ROWS, HID), F32),
            jax.ShapeDtypeStruct((HID, HID), F32),
        ),
        in_specs=[pl.BlockSpec(memory_space=pltpu.SMEM), hbm, vmem, vmem, hbm],
        out_specs=(vmem, vmem, vmem),
        scratch_shapes=scratch,
        compiler_params=pltpu.CompilerParams(
            collective_id=0, has_side_effects=True, vmem_limit_bytes=48 << 20
        ),
        name="graph_layer",
    )(inv, features, weight, cotangent, tiles)


def body(features, weight, cotangent, tile_values, tile_pos, tile_count):
    pos_here = tile_pos[0, 0]
    slots = jnp.arange(KMAX, dtype=jnp.int32)
    live = slots < tile_count[0, 0]
    places = jnp.arange(TILE, dtype=jnp.int32)
    hit = (pos_here[None, :] == places[:, None]) & live[None, :]
    inv = KMAX + jnp.sum(jnp.where(hit, slots[None, :] - KMAX, 0), axis=1)
    return layer(inv, features, weight, cotangent, tile_values[0, 0])


def solution(mesh):
    in_specs = (
        P(("row", "rep"), None),
        P(),
        P(("row", "rep"), None),
        P("row", "rep", None, None, None),
        P("row", "rep", None),
        P("row", "rep"),
    )
    out_specs = (P(("row", "rep"), None), P(("row", "rep"), None), P())
    return jax.shard_map(body, mesh=mesh, in_specs=in_specs, out_specs=out_specs, check_vma=False)
```

time: 572 us -> 99.7 us (0.17)
  waiting for transfers between devices: 463 us -> 0 us
  Pallas kernels: 0 us -> 90.7 us
  matrix products: 39.2 us -> 0 us
  starting transfers between devices: 22.2 us -> 0 us
  local copies, waits for them, and re-layouts: 25.3 us -> 6.69 us
  between operations: 14.6 us -> 1.31 us
  other arithmetic: 6.82 us -> 0.77 us
    psum x1 -> x0, waiting for transfers between devices: 253 us -> none  [body(): grad_weight = lax.psum(local_weight, ('row', 'rep')) / math.sqrt(node_total)]
    reduce_scatter x1 -> x0, waiting for transfers between devices: 102 us -> none  [body(): lax.psum_scatter(summed.reshape(lax.axis_size('rep') * share_rows, HID),...]
    pallas_call x0 -> x1, Pallas kernels: none -> 90.7 us  [layer(): pl.pallas_call(kernel, out_shape=(jax.ShapeDtypeStruct((ROWS, HID), F32),...]
    all_gather x1 -> x0, waiting for transfers between devices: 77.8 us -> none  [body(): lax.all_gather(back_share, 'rep', axis=0, tiled=True)]
    dot_general x7 -> x0, matrix products: 39.2 us -> none  [the longest x1 12.7 us: body(): jnp.einsum('kij,kjh->kih', values_here, picked, precision=lax.Precision.H...]
    ppermute x6 -> x0, waiting for transfers between devices: 31.1 us -> none  [passed_along(): return lax.ppermute(block, axis, route)]
    ppermute x6 -> x0, starting transfers between devices: 21.9 us -> none  [passed_along(): return lax.ppermute(block, axis, route)]
    dot_general x3 -> x0, local copies, waits for them, and re-layouts: 14.9 us -> none  [the longest x1 6.16 us: body(): jnp.einsum('kji,kjh->kih', values_here, picked_back, precision=lax.Precis...]
  transfers between devices with their start and end apart: 9 -> 0, of which waited for: 8 -> 0; matrix products, arithmetic and copies ran while one was open for 1% -> 0% of each run, Pallas kernels for 0% -> 0%
where the time goes in v1:
time: 99.7 us; the launch traced here: 99.5 us
  Pallas kernels  90.7 us (91%)
  local copies, waits for them, and re-layouts  6.69 us (7%)
  between operations  1.31 us (1%)
    pallas_call x1, Pallas kernels, layer(): pl.pallas_call(kernel, out_shape=(jax.ShapeDtypeStruct((ROWS, HID), F32),...  90.7 us
    unnamed x11, local copies, waits for them, and re-layouts  6.69 us

profile of v1, /device:TPU:1, one launch (start us, length us, event | category | flops | bytes accessed | tf_op | source)
XLA Modules:
  0.0 99.5 jit_solution(7504091193775088041)
XLA Ops:
  1.3 0.8 select_reduce_fusion
  2.1 0.0 copy-start
  2.1 1.7 %copy-done = f32[1,1,40,128,128]{4,3,2,1,0:T(8,128)S(1)} copy-done((f32[1,1,40,128,128]{4,3,2,1,0:T(8,128)S(1)}, f32[1,1,40,128,128]{4,3,2,1,0:T(8,128)}, u32[]{:S(2)}) %copy-start) | copy-done | bytes 2621464
  3.8 0.0 copy-start.1
  3.8 0.9 copy-done.1
  4.8 0.0 copy-start.2
  4.8 0.9 copy-done.2
  5.7 0.0 copy-start.3
  5.7 0.9 copy-done.3
  6.7 90.7 %graph_layer.1 = (f32[256,256]{1,0:T(8,128)S(1)}, f32[256,256]{1,0:T(8,128)S(1)}, f32[256,256]{1,0:T(8,128)S(1)}) custom-call(s32[128]{0:T(128)S(1)} %broadcast_add_fusion.inv, f32[256,256]{1,0:T(8,128)S(1)} %copy-done.1, f32[256,256]{1,0:T(8,128)S(1)} %copy-done.2, f32[256,256]{1,0:T(8,128)S(1)} %copy-done.3, f32[40,128,128]{2,1,0:T(8,128)S(1)} %bitcast.4), custom_call_target="tpu_custom_call" | custom-call | tf_op jit(solution)/shard_map/graph_layer/pallas_call | solution.py:427
  97.4 0.7 copy.13
  98.1 0.7 copy.14
  98.8 0.7 copy.15
  (3 shorter events, 0.0 us)
Async XLA Ops:
  2.1 1.7 %copy-start = (f32[1,1,40,128,128]{4,3,2,1,0:T(8,128)S(1)}, f32[1,1,40,128,128]{4,3,2,1,0:T(8,128)}, u32[]{:S(2)}) copy-start(f32[1,1,40,128,128]{4,3,2,1,0:T(8,128)} %param.9) | copy-start | bytes 7864324
  3.8 0.9 copy-start.1
  4.8 0.9 copy-start.2
  5.7 0.9 copy-start.3

commit v2 on v1

v2 whole, which is shorter than its diff:
```python
import functools
import math

import jax
import jax.numpy as jnp
from jax import lax
from jax.experimental import pallas as pl
from jax.experimental.pallas import tpu as pltpu
from jax.sharding import PartitionSpec as P

HID = 256
TILE = 128
STOPS = 4
KMAX = 40
ROWS = 256
HALF = 128
NX = 4
NY = 8
NZ = 8
SLABS = 64
MESH = pl.DeviceIdType.MESH
BF = jnp.bfloat16
F32 = jnp.float32


def split(value):
    high = value.astype(BF)
    low = (value - high.astype(F32)).astype(BF)
    return high, low


def dot(a, b, contract=((1,), (0,))):
    return lax.dot_general(a, b, (contract, ((), ())), preferred_element_type=F32)


def dot3(a, b, contract=((1,), (0,))):
    a_hi, a_lo = a
    b_hi, b_lo = b
    return dot(a_hi, b_hi, contract) + (dot(a_hi, b_lo, contract) + dot(a_lo, b_hi, contract))


def kernel(
    pos, count, feat, weight_hbm, cot_hbm, tiles_hbm, act_hbm, gf_hbm, gw_hbm,
    act, gf, tiles, inv_row, inv, weight, w_hi, w_lo, cot, slopes, a_hi, a_lo, t_hi, t_lo, band, x_cat,
    pbuf, rx1, rx2, zsend, zrecv, mine, g, sp, rr, lw, cr, yr, xr, zz, wh, gwb,
    load_sem, store_sem, band_s, band_r, rs_s, rs_r, zx_s, zx_r, ag_s, ag_r, az_s, az_r,
    ring_s, ring_r, red_s, red_r,
):
    row = lax.axis_index("row")
    rep = lax.axis_index("rep")
    core = lax.rem(row, 2)
    y = lax.rem(row // 2, NY)
    z_lo = row // 16
    x = rep // 2
    z_hi = lax.rem(rep, 2)
    z = z_hi * 4 + z_lo

    def device(core_, y_, z_, x_):
        return (lax.rem(z_, 4) * 16 + y_ * 2 + core_, x_ * 2 + z_ // 4)

    x_right = lax.rem(x + 1, NX)
    x_opp = lax.rem(x + 2, NX)
    x_left = lax.rem(x + 3, NX)
    right = (row, x_right * 2 + z_hi)
    left = (row, x_left * 2 + z_hi)
    across = (row, x * 2 + 1 - z_hi)
    partner = (row + 1 - 2 * core, rep)
    following = (lax.rem(row + 1, SLABS), rep)
    previous = (lax.rem(row + SLABS - 1, SLABS), rep)
    y_peers = [device(core, lax.rem(y + k, NY), z, x) for k in range(1, NY)]
    x_peers = [device(core, y, z, lax.rem(x + k, NX)) for k in range(1, NX)]
    z_peers = [device(core, y, lax.rem(z + k, NZ), x) for k in range(1, NZ)]

    started = []
    stores = []

    def store(src, dst, k):
        copy = pltpu.make_async_copy(src, dst, store_sem.at[k])
        copy.start()
        stores.append(copy)

    def send(src, dst, s_sem, r_sem, to):
        copy = pltpu.make_async_remote_copy(
            src_ref=src, dst_ref=dst, send_sem=s_sem, recv_sem=r_sem,
            device_id=to, device_id_type=MESH,
        )
        copy.start()
        started.append(copy)
        return copy

    barrier = pltpu.get_barrier_semaphore()
    greeted = [following, previous, partner] + y_peers + x_peers + z_peers
    for peer in greeted:
        pl.semaphore_signal(barrier, inc=1, device_id=peer, device_id_type=MESH)

    loads = [
        pltpu.make_async_copy(tiles_hbm.at[0, 0], tiles.at[pl.ds(0, KMAX)], load_sem.at[0]),
        pltpu.make_async_copy(feat.at[:, pl.ds(0, HALF)], band.at[0, 0], load_sem.at[1]),
        pltpu.make_async_copy(feat.at[:, pl.ds(HALF, HALF)], band.at[0, 1], load_sem.at[2]),
        pltpu.make_async_copy(weight_hbm, weight, load_sem.at[3]),
        pltpu.make_async_copy(cot_hbm, cot, load_sem.at[4]),
    ]
    for copy in loads:
        copy.start()

    lanes = lax.broadcasted_iota(jnp.int32, (1, TILE), 1)
    found = jnp.full((1, TILE), KMAX, jnp.int32)
    for k in range(KMAX):
        place = jnp.where(k < count[0, 0], pos[0, 0, k], -1)
        found = jnp.where(lanes == place, k, found)
    inv_row[...] = found
    to_scalars = pltpu.make_async_copy(inv_row, inv, load_sem.at[5])
    to_scalars.start()
    tiles[KMAX] = jnp.zeros((TILE, TILE), F32)
    pl.semaphore_wait(barrier, len(greeted))

    band_copy = {}

    def band_send(s, c):
        for h in range(2):
            rows = pl.ds(h * HALF, HALF)
            src = band.at[s, c, rows] if s > 0 else feat.at[rows, pl.ds(c * HALF, HALF)]
            band_copy[s, c, h] = send(
                src, band.at[s + 1, c, rows], band_s.at[s, c, h], band_r.at[s, c, h], following
            )

    def band_take(s, c):
        high, low = split(band[s, c])
        x_cat[c, s * ROWS:(s + 1) * ROWS, 0:HALF] = high
        x_cat[c, s * ROWS:(s + 1) * ROWS, HALF:2 * HALF] = low

    def band_step(s, c):
        for h in range(2):
            band_copy[s, c, h].wait_recv()
            if s + 1 < STOPS - 1:
                rows = pl.ds(h * HALF, HALF)
                band_copy[s + 1, c, h] = send(
                    band.at[s + 1, c, rows], band.at[s + 2, c, rows],
                    band_s.at[s + 1, c, h], band_r.at[s + 1, c, h], following,
                )
        band_take(s + 1, c)

    band_send(0, 0)
    to_scalars.wait()
    for copy in loads[:3]:
        copy.wait()
    band_take(0, 0)
    band_take(0, 1)

    def fill_rows(x_at, own, half):
        d = x_at * 2 + (z_hi if own else 1 - z_hi)
        for q in range(8):
            tile = tiles[inv[0, (d * 2 + half) * 8 + q]]
            high, low = split(tile)
            a_hi[d, half * TILE:(half + 1) * TILE, q * TILE:(q + 1) * TILE] = high
            a_lo[d, half * TILE:(half + 1) * TILE, q * TILE:(q + 1) * TILE] = low

    def fill_all(own, half):
        def one(i, carry):
            fill_rows(lax.rem(x + i, NX), own, half)
            return carry

        lax.fori_loop(0, NX, one, 0)

    def fill_turned(i, carry):
        d = i // STOPS
        s = lax.rem(i, STOPS)
        for tt in range(2):
            for j in range(2):
                tile = tiles[inv[0, (d * 2 + tt) * 8 + s * 2 + j]]
                high, low = split(tile.T)
                t_hi[d, s, j * TILE:(j + 1) * TILE, tt * TILE:(tt + 1) * TILE] = high
                t_lo[d, s, j * TILE:(j + 1) * TILE, tt * TILE:(tt + 1) * TILE] = low
        return carry

    def turn(part):
        lax.fori_loop(part * 8, part * 8 + 8, fill_turned, 0)

    fill_all(0, 0)
    band_step(0, 0)
    band_send(0, 1)
    fill_all(0, 1)
    band_step(1, 0)
    band_step(0, 1)
    band_step(2, 0)

    rs_copy = {}

    def partial_rows(u, place, x_to, c):
        own, half = u // 2, u % 2
        d = x_to * 2 + (z_hi if own else 1 - z_hi)
        rows = pl.ds(half * HALF, HALF)
        both = dot(a_hi[d, rows], x_cat[c])
        rest = dot(a_lo[d, rows], x_cat[c, :, 0:HALF])
        pbuf[u, place, c] = both[:, 0:HALF] + (both[:, HALF:2 * HALF] + rest)

    def rs_send(u, k, src, dst, to):
        rs_copy[u, k] = send(src, dst, rs_s.at[u, k], rs_r.at[u, k], to)

    def rs_begin(u, c):
        partial_rows(u, 0, x_opp, c)
        if c == 0:
            rs_send(u, 0, pbuf.at[u, 0, 0], rx1.at[u, 0], right)
            partial_rows(u, 2, x_left, 0)
            rs_send(u, 2, pbuf.at[u, 2, 0], rx2.at[u, 1, 0], left)
            partial_rows(u, 1, x_right, 0)
        else:
            rs_send(u, 1, pbuf.at[u, 0, 1], rx1.at[u, 1], left)
            partial_rows(u, 1, x_right, 1)
            rs_send(u, 3, pbuf.at[u, 1, 1], rx2.at[u, 0, 1], right)
            partial_rows(u, 2, x_left, 1)
        partial_rows(u, 3, x, c)

    def rs_relay(u, c):
        rs_copy[u, c].wait_recv()
        place, to = (1, right) if c == 0 else (2, left)
        pbuf[u, place, c] = pbuf[u, place, c] + rx1[u, c]
        rs_send(u, 4 + c, pbuf.at[u, place, c], rx2.at[u, c, c], to)

    zx_copy = {}

    def rs_finish(u):
        own, half = u // 2, u % 2
        for k in (2, 3, 4, 5):
            rs_copy[u, k].wait_recv()
        if own:
            zx_copy[half].wait_recv()
        for c in range(2):
            total = pbuf[u, 3, c] + (rx2[u, 0, c] + rx2[u, 1, c])
            if own:
                mine[half * HALF:(half + 1) * HALF, c * HALF:(c + 1) * HALF] = total + zrecv[half, c]
            else:
                zsend[half, c] = total
        if not own:
            zx_copy[half] = send(
                zsend.at[half], zrecv.at[half], zx_s.at[half], zx_r.at[half], across
            )

    ag_copy = {}
    az_copy = {}
    taken = set()

    def place_of(own, x_at):
        return x_at * 2 + (z_hi if own else 1 - z_hi)

    def ag_send(own, h, c, k, src, to):
        ag_copy[own, h, c, k] = send(src, src, ag_s.at[own, h, c, k], ag_r.at[own, h, c, k], to)

    def ag_take(own, h, c, k):
        if (own, h, c, k) not in taken:
            taken.add((own, h, c, k))
            ag_copy[own, h, c, k].wait_recv()

    def ag_relay(own, h, c):
        if (c if own else h) == 0:
            ag_take(own, h, c, 0)
            ag_send(own, h, c, 2, g.at[place_of(own, x_left), h, c], right)
        else:
            ag_take(own, h, c, 1)
            ag_send(own, h, c, 2, g.at[place_of(own, x_right), h, c], left)

    def ag_across(h, c):
        az_copy[h, c].wait_recv()
        block = g.at[place_of(0, x), h, c]
        ag_send(0, h, c, 0, block, right)
        ag_send(0, h, c, 1, block, left)

    def share_rows(h):
        rows = pl.ds(h * HALF, HALF)
        preact = dot3(split(mine[rows, :]), (w_hi[...], w_lo[...]))
        squashed = jax.nn.sigmoid(preact)
        slope = cot[rows, :] * squashed * (1.0 + preact * (1.0 - squashed))
        s_parts = split(slope)
        for c in range(2):
            columns = slice(c * HALF, (c + 1) * HALF)
            g[rep, h, c] = dot3(s_parts, (w_hi[columns, :], w_lo[columns, :]), ((1,), (1,)))
            block = g.at[rep, h, c]
            az_copy[h, c] = send(block, block, az_s.at[h, c], az_r.at[h, c], across)
            if c == 0:
                ag_send(1, h, 0, 0, block, right)
        ag_send(1, h, 1, 1, g.at[rep, h, 1], left)
        ag_send(1, h, 1, 0, g.at[rep, h, 1], right)
        ag_send(1, h, 0, 1, g.at[rep, h, 0], left)
        act[rows, :] = preact * squashed
        store(act.at[rows], act_hbm.at[rows], h)
        slopes[rows, :] = slope

    rs_begin(0, 0)
    band_step(1, 1)
    rs_begin(1, 0)
    band_step(2, 1)
    rs_begin(0, 1)
    rs_relay(0, 0)
    rs_begin(1, 1)
    rs_relay(0, 1)
    rs_relay(1, 0)
    fill_all(1, 0)
    rs_relay(1, 1)
    rs_begin(2, 0)
    rs_begin(2, 1)
    rs_finish(0)
    fill_all(1, 1)
    rs_relay(2, 0)
    rs_relay(2, 1)
    rs_begin(3, 0)
    rs_finish(1)
    rs_begin(3, 1)
    loads[3].wait()
    loads[4].wait()
    w_hi[...], w_lo[...] = split(weight[...])
    turn(0)
    rs_relay(3, 0)
    rs_relay(3, 1)
    rs_finish(2)
    share_rows(0)
    turn(1)
    turn(2)
    rs_finish(3)
    ag_relay(1, 0, 0)
    ag_relay(1, 0, 1)
    share_rows(1)

    red_copy = {}

    def red_send(k, src, dst, to):
        red_copy[k] = send(src, dst, red_s.at[k], red_r.at[k], to)

    turned = split(mine[...].T)
    s_parts = split(slopes[...])
    for c in range(2):
        lw[c] = dot3(turned, (s_parts[0][:, c * HALF:(c + 1) * HALF], s_parts[1][:, c * HALF:(c + 1) * HALF]))
    red_send(0, lw.at[1 - core], cr, partner)
    turn(3)

    def red_y():
        red_copy[0].wait_recv()
        lw[core] = lw[core] + cr[...]
        for k in range(1, NY):
            rows = pl.ds(pl.multiple_of(lax.rem(y + k, NY) * 32, 32), 32)
            red_send(k, lw.at[core, rows], yr.at[y], y_peers[k - 1])
        yr[y] = lw[core, pl.ds(pl.multiple_of(y * 32, 32), 32)]

    def red_x():
        for k in range(1, NY):
            red_copy[k].wait_recv()
        yr[0] = jnp.sum(yr[...], axis=0)
        for k in range(1, NX):
            rows = pl.ds(pl.multiple_of(lax.rem(x + k, NX) * 8, 8), 8)
            red_send(7 + k, yr.at[0, rows], xr.at[x], x_peers[k - 1])
        xr[x] = yr[0, pl.ds(pl.multiple_of(x * 8, 8), 8)]

    def red_z():
        for k in range(1, NX):
            red_copy[7 + k].wait_recv()
        zz[z] = jnp.sum(xr[...], axis=0)
        for k in range(1, NZ):
            red_send(10 + k, zz.at[z], zz.at[z], z_peers[k - 1])

    def red_x_back():
        for k in range(1, NZ):
            red_copy[10 + k].wait_recv()
        rows = pl.ds(pl.multiple_of(y * 32 + x * 8, 8), 8)
        wh[rows] = jnp.sum(zz[...], axis=0) * (1.0 / math.sqrt(SLABS * 8 * ROWS))
        for k in range(1, NX):
            red_send(17 + k, wh.at[rows], wh.at[rows], x_peers[k - 1])

    def red_y_back():
        for k in range(1, NX):
            red_copy[17 + k].wait_recv()
        rows = pl.ds(pl.multiple_of(y * 32, 32), 32)
        for k in range(1, NY):
            red_send(20 + k, wh.at[rows], wh.at[rows], y_peers[k - 1])

    def red_core_back():
        for k in range(1, NY):
            red_copy[20 + k].wait_recv()
        gwb[core] = wh[...]
        red_send(28, gwb.at[core], gwb.at[core], partner)

    def spread_begin(d, c):
        for h in range(2):
            rows = slice(h * HALF, (h + 1) * HALF)
            high, low = split(g[d, h, c])
            x_cat[c, rows, 0:HALF] = high
            x_cat[c, rows, HALF:2 * HALF] = low

    def spread_stop(d, c, s, first=False):
        both = dot(t_hi[d, s], x_cat[c, 0:ROWS])
        rest = dot(t_lo[d, s], x_cat[c, 0:ROWS, 0:HALF])
        term = both[:, 0:HALF] + (both[:, HALF:2 * HALF] + rest)
        sp[c, s] = term if first else sp[c, s] + term

    def spread(own, x_at, c, first=False):
        d = place_of(own, x_at)
        spread_begin(d, c)

        def one_stop(s, carry):
            spread_stop(d, c, s, first)
            return carry

        lax.fori_loop(0, STOPS, one_stop, 0)

    def spread_sides(own, c):
        for k, x_at in ((1, x_right), (0, x_left)):
            for h in range(2):
                ag_take(own, h, c, k)
            spread(own, x_at, c)

    def spread_opposite(own, c):
        for h in range(2):
            ag_take(own, h, c, 2)
        if own:
            spread(own, x_opp, c)
            return
        d = place_of(own, x_opp)
        spread_begin(d, c)
        spread_stop(d, c, STOPS - 1)
        ring_send(c, 0, 0)
        ring_send(c, 0, 1)

        def one_stop(i, carry):
            spread_stop(d, c, STOPS - 2 - i)
            return carry

        lax.fori_loop(0, STOPS - 1, one_stop, 0)

    ring_copy = {}

    def ring_send(c, step, h):
        rows = pl.ds(h * HALF, HALF)
        ring_copy[c, step, h] = send(
            sp.at[c, STOPS - 1 - step, rows], rr.at[step, c, rows],
            ring_s.at[c, step, h], ring_r.at[c, step, h], previous,
        )

    def ring_step(c, step):
        s = STOPS - 2 - step
        for h in range(2):
            ring_copy[c, step, h].wait_recv()
            rows = pl.ds(h * HALF, HALF)
            if s > 0:
                sp[c, s, rows] = sp[c, s, rows] + rr[step, c, rows]
                ring_send(c, step + 1, h)
            else:
                gf[c, rows] = sp[c, 0, rows] + rr[step, c, rows]
        if s == 0:
            store(gf.at[c], gf_hbm.at[:, pl.ds(c * HALF, HALF)], 2 + c)

    ag_across(0, 0)
    spread(1, x, 0, first=True)
    ag_relay(1, 1, 0)
    ag_relay(1, 1, 1)
    red_y()
    spread(1, x, 1, first=True)
    ag_across(0, 1)
    spread_sides(1, 0)
    ag_relay(0, 0, 0)
    spread_sides(1, 1)
    ag_across(1, 0)
    spread(0, x, 0)
    spread_opposite(1, 0)
    ag_relay(0, 0, 1)
    red_x()
    spread_opposite(1, 1)
    ag_across(1, 1)
    ag_relay(0, 1, 0)
    spread(0, x, 1)
    spread_sides(0, 0)
    ag_relay(0, 1, 1)
    spread_opposite(0, 0)
    red_z()
    spread_sides(0, 1)
    ring_step(0, 0)
    spread_opposite(0, 1)
    red_x_back()
    ring_step(0, 1)
    ring_step(1, 0)
    red_y_back()
    ring_step(0, 2)
    ring_step(1, 1)
    red_core_back()
    ring_step(1, 2)
    red_copy[28].wait_recv()
    for c in range(2):
        store(gwb.at[c], gw_hbm.at[:, pl.ds(c * HALF, HALF)], 4 + c)
    for copy in stores:
        copy.wait()
    for copy in started:
        copy.wait_send()


def write_out(act, gf, gw, act_out, gf_out, gw_out, held, sems):
    for first, refs in ((0, (act, gf, gw)), (3, (act_out, gf_out, gw_out))):
        copies = [
            pltpu.make_async_copy(ref, held.at[i], sems.at[first + i])
            if first == 0
            else pltpu.make_async_copy(held.at[i], ref, sems.at[first + i])
            for i, ref in enumerate(refs)
        ]
        for copy in copies:
            copy.start()
        for copy in copies:
            copy.wait()


def layer(pos, count, features, weight, cotangent, tiles):
    smem = pl.BlockSpec(memory_space=pltpu.SMEM)
    hbm = pl.BlockSpec(memory_space=pltpu.HBM)
    dma = lambda *shape: pltpu.SemaphoreType.DMA(shape)
    block = (ROWS, HALF)
    piece = (HALF, HALF)
    scratch = [
        pltpu.VMEM((ROWS, HID), F32),
        pltpu.VMEM((2,) + block, F32),
        pltpu.VMEM((KMAX + 1, TILE, TILE), F32),
        pltpu.VMEM((1, TILE), jnp.int32),
        pltpu.SMEM((1, TILE), jnp.int32),
        pltpu.VMEM((HID, HID), F32),
        pltpu.VMEM((HID, HID), BF),
        pltpu.VMEM((HID, HID), BF),
        pltpu.VMEM((ROWS, HID), F32),
        pltpu.VMEM((ROWS, HID), F32),
        pltpu.VMEM((8, ROWS, STOPS * ROWS), BF),
        pltpu.VMEM((8, ROWS, STOPS * ROWS), BF),
        pltpu.VMEM((8, STOPS, ROWS, ROWS), BF),
        pltpu.VMEM((8, STOPS, ROWS, ROWS), BF),
        pltpu.VMEM((STOPS, 2) + block, F32),
        pltpu.VMEM((2, STOPS * ROWS, 2 * HALF), BF),
        pltpu.VMEM((4, 4, 2) + piece, F32),
        pltpu.VMEM((4, 2) + piece, F32),
        pltpu.VMEM((4, 2, 2) + piece, F32),
        pltpu.VMEM((2, 2) + piece, F32),
        pltpu.VMEM((2, 2) + piece, F32),
        pltpu.VMEM((ROWS, HID), F32),
        pltpu.VMEM((8, 2, 2) + piece, F32),
        pltpu.VMEM((2, STOPS) + block, F32),
        pltpu.VMEM((STOPS - 1, 2) + block, F32),
        pltpu.VMEM((2,) + block, F32),
        pltpu.VMEM(block, F32),
        pltpu.VMEM((NY, 32, HALF), F32),
        pltpu.VMEM((NX, 8, HALF), F32),
        pltpu.VMEM((NZ, 8, HALF), F32),
        pltpu.VMEM(block, F32),
        pltpu.VMEM((2,) + block, F32),
        dma(6), dma(6),
        dma(3, 2, 2), dma(3, 2, 2),
        dma(4, 6), dma(4, 6),
        dma(2), dma(2),
        dma(2, 2, 2, 3), dma(2, 2, 2, 3),
        dma(2, 2), dma(2, 2),
        dma(2, 3, 2), dma(2, 3, 2),
        dma(29), dma(29),
    ]
    outs = (
        jax.ShapeDtypeStruct((ROWS, HID), F32),
        jax.ShapeDtypeStruct((ROWS, HID), F32),
        jax.ShapeDtypeStruct((HID, HID), F32),
    )
    parts = pl.pallas_call(
        kernel,
        out_shape=outs,
        in_specs=[smem, smem, hbm, hbm, hbm, hbm],
        out_specs=(hbm, hbm, hbm),
        scratch_shapes=scratch,
        compiler_params=pltpu.CompilerParams(
            collective_id=0, has_side_effects=True, vmem_limit_bytes=60 << 20
        ),
        name="graph_layer",
    )(pos, count, features, weight, cotangent, tiles)
    return pl.pallas_call(
        write_out,
        out_shape=outs,
        in_specs=[hbm, hbm, hbm],
        out_specs=(hbm, hbm, hbm),
        scratch_shapes=[pltpu.VMEM((3, ROWS, HID), F32), dma(6)],
        compiler_params=pltpu.CompilerParams(vmem_limit_bytes=60 << 20),
        name="write_out",
    )(*parts)


def body(features, weight, cotangent, tile_values, tile_pos, tile_count):
    return layer(tile_pos, tile_count, features, weight, cotangent, tile_values)


def solution(mesh):
    in_specs = (
        P(("row", "rep"), None),
        P(),
        P(("row", "rep"), None),
        P("row", "rep", None, None, None),
        P("row", "rep", None),
        P("row", "rep"),
    )
    out_specs = (P(("row", "rep"), None), P(("row", "rep"), None), P())
    return jax.shard_map(body, mesh=mesh, in_specs=in_specs, out_specs=out_specs, check_vma=False)
```

time: 99.7 us -> 91.2 us (0.915)
  local copies, waits for them, and re-layouts: 6.69 us -> 0 us
    unnamed x11 -> x0, local copies, waits for them, and re-layouts: 6.69 us -> none
    pallas_call x1 -> x2, Pallas kernels: 90.7 us -> 89.8 us  [the longest x1 87.7 us: layer(): pl.pallas_call(kernel, out_shape=outs, in_specs=[smem, smem, hbm, hbm, hb...]
where the time goes in v2:
time: 91.2 us; the launch traced here: 91.1 us
  Pallas kernels  89.8 us (98%)
  between operations  1.29 us (1%)
    pallas_call x1, Pallas kernels, layer(): pl.pallas_call(kernel, out_shape=outs, in_specs=[smem, smem, hbm, hbm, hb...  87.7 us
    pallas_call x1, Pallas kernels, layer(): pl.pallas_call(write_out, out_shape=outs, in_specs=[hbm, hbm, hbm], out_s...  2.03 us

profile of v2, /device:TPU:1, one launch (start us, length us, event | category | flops | bytes accessed | tf_op | source)
XLA Modules:
  0.0 91.1 jit_solution(5950447931056993187)
XLA Ops:
  1.3 87.7 %graph_layer.1 = (f32[256,256]{1,0:T(8,128)}, f32[256,256]{1,0:T(8,128)}, f32[256,256]{1,0:T(8,128)}) custom-call(s32[1,1,40]{2,1,0:T(1,128)} %pos.1, s32[1,1]{1,0:T(1,128)S(6)} %copy.9.count, f32[256,256]{1,0:T(8,128)} %feat.1, f32[256,256]{1,0:T(8,128)} %weight_hbm.1, f32[256,256]{1,0:T(8,128)} %cot_hbm.1, f32[1,1,40,128,128]{4,3,2,1,0:T(8,128)} %tiles_hbm.1), custom_call_target="tpu_custom_call" | custom-call | tf_op jit(solution)/shard_map/graph_layer/pallas_call | solution.py:559
  89.0 2.0 %write_out.1 = (f32[256,256]{1,0:T(8,128)}, f32[256,256]{1,0:T(8,128)}, f32[256,256]{1,0:T(8,128)}) custom-call(f32[256,256]{1,0:T(8,128)} %get-tuple-element.6.act, f32[256,256]{1,0:T(8,128)} %get-tuple-element.7.gf, f32[256,256]{1,0:T(8,128)} %get-tuple-element.8.gw), custom_call_target="tpu_custom_call" | custom-call | tf_op jit(solution)/shard_map/write_out/pallas_call | solution.py:570

commit v3 on v2

--- a/solution.py
+++ b/solution.py
@@ -14,6 +14,7 @@
 KMAX = 40
 ROWS = 256
 HALF = 128
+BAND = STOPS * ROWS
 NX = 4
 NY = 8
 NZ = 8
@@ -41,8 +42,8 @@
 
 def kernel(
     pos, count, feat, weight_hbm, cot_hbm, tiles_hbm, act_hbm, gf_hbm, gw_hbm,
-    act, gf, tiles, inv_row, inv, weight, w_hi, w_lo, cot, slopes, a_hi, a_lo, t_hi, t_lo, band, x_cat,
-    pbuf, rx1, rx2, zsend, zrecv, mine, g, sp, rr, lw, cr, yr, xr, zz, wh, gwb,
+    act, gf, tiles, inv_row, inv, weight, w_hi, w_lo, cot, slopes, a_cat, t_cat, band, x_cat,
+    pbuf, rx1, rx2, zsend, zrecv, mine, g, acc, sp, rr, lw, cr, yr, xr, zz, wh, gwb,
     load_sem, store_sem, band_s, band_r, rs_s, rs_r, zx_s, zx_r, ag_s, ag_r, az_s, az_r,
     ring_s, ring_r, red_s, red_r,
 ):
@@ -124,10 +125,15 @@
                 src, band.at[s + 1, c, rows], band_s.at[s, c, h], band_r.at[s, c, h], following
             )
 
+    def put_parts(c, start, value, gap):
+        high, low = split(value)
+        rows = value.shape[0]
+        for first in (start, start + gap):
+            x_cat[c, first:first + rows, 0:HALF] = high
+            x_cat[c, first:first + rows, HALF:2 * HALF] = low
+
     def band_take(s, c):
-        high, low = split(band[s, c])
-        x_cat[c, s * ROWS:(s + 1) * ROWS, 0:HALF] = high
-        x_cat[c, s * ROWS:(s + 1) * ROWS, HALF:2 * HALF] = low
+        put_parts(c, s * ROWS, band[s, c], BAND)
 
     def band_step(s, c):
         for h in range(2):
@@ -152,8 +158,9 @@
         for q in range(8):
             tile = tiles[inv[0, (d * 2 + half) * 8 + q]]
             high, low = split(tile)
-            a_hi[d, half * TILE:(half + 1) * TILE, q * TILE:(q + 1) * TILE] = high
-            a_lo[d, half * TILE:(half + 1) * TILE, q * TILE:(q + 1) * TILE] = low
+            rows = slice(half * TILE, (half + 1) * TILE)
+            a_cat[d, rows, q * TILE:(q + 1) * TILE] = high
+            a_cat[d, rows, BAND + q * TILE:BAND + (q + 1) * TILE] = low
 
     def fill_all(own, half):
         def one(i, carry):
@@ -169,8 +176,9 @@
             for j in range(2):
                 tile = tiles[inv[0, (d * 2 + tt) * 8 + s * 2 + j]]
                 high, low = split(tile.T)
-                t_hi[d, s, j * TILE:(j + 1) * TILE, tt * TILE:(tt + 1) * TILE] = high
-                t_lo[d, s, j * TILE:(j + 1) * TILE, tt * TILE:(tt + 1) * TILE] = low
+                rows = pl.ds(pl.multiple_of(s * ROWS + j * TILE, TILE), TILE)
+                t_cat[d, rows, tt * TILE:(tt + 1) * TILE] = high
+                t_cat[d, rows, ROWS + tt * TILE:ROWS + (tt + 1) * TILE] = low
         return carry
 
     def turn(part):
@@ -187,12 +195,10 @@
     rs_copy = {}
 
     def partial_rows(u, place, x_to, c):
-        own, half = u // 2, u % 2
-        d = x_to * 2 + (z_hi if own else 1 - z_hi)
-        rows = pl.ds(half * HALF, HALF)
-        both = dot(a_hi[d, rows], x_cat[c])
-        rest = dot(a_lo[d, rows], x_cat[c, :, 0:HALF])
-        pbuf[u, place, c] = both[:, 0:HALF] + (both[:, HALF:2 * HALF] + rest)
+        d = x_to * 2 + (z_hi if u // 2 else 1 - z_hi)
+        half = u % 2
+        both = dot(a_cat[d, half * HALF:(half + 1) * HALF], x_cat[c])
+        pbuf[u, place, c] = both[:, 0:HALF] + both[:, HALF:2 * HALF]
 
     def rs_send(u, k, src, dst, to):
         rs_copy[u, k] = send(src, dst, rs_s.at[u, k], rs_r.at[u, k], to)
@@ -297,13 +303,13 @@
     fill_all(1, 0)
     rs_relay(1, 1)
     rs_begin(2, 0)
+    rs_finish(0)
     rs_begin(2, 1)
-    rs_finish(0)
     fill_all(1, 1)
+    rs_finish(1)
     rs_relay(2, 0)
     rs_relay(2, 1)
     rs_begin(3, 0)
-    rs_finish(1)
     rs_begin(3, 1)
     loads[3].wait()
     loads[4].wait()
@@ -315,6 +321,7 @@
     share_rows(0)
     turn(1)
     turn(2)
+    turn(3)
     rs_finish(3)
     ag_relay(1, 0, 0)
     ag_relay(1, 0, 1)
@@ -330,7 +337,6 @@
     for c in range(2):
         lw[c] = dot3(turned, (s_parts[0][:, c * HALF:(c + 1) * HALF], s_parts[1][:, c * HALF:(c + 1) * HALF]))
     red_send(0, lw.at[1 - core], cr, partner)
-    turn(3)
 
     def red_y():
         red_copy[0].wait_recv()
@@ -340,65 +346,51 @@
             red_send(k, lw.at[core, rows], yr.at[y], y_peers[k - 1])
         yr[y] = lw[core, pl.ds(pl.multiple_of(y * 32, 32), 32)]
 
-    def red_x():
+    def red_z():
         for k in range(1, NY):
             red_copy[k].wait_recv()
-        yr[0] = jnp.sum(yr[...], axis=0)
+        zz[z] = jnp.sum(yr[...], axis=0)
+        for k in range(1, NZ):
+            red_send(7 + k, zz.at[z], zz.at[z], z_peers[k - 1])
+
+    def red_x():
+        for k in range(1, NZ):
+            red_copy[7 + k].wait_recv()
+        xr[x] = jnp.sum(zz[...], axis=0)
         for k in range(1, NX):
-            rows = pl.ds(pl.multiple_of(lax.rem(x + k, NX) * 8, 8), 8)
-            red_send(7 + k, yr.at[0, rows], xr.at[x], x_peers[k - 1])
-        xr[x] = yr[0, pl.ds(pl.multiple_of(x * 8, 8), 8)]
-
-    def red_z():
-        for k in range(1, NX):
-            red_copy[7 + k].wait_recv()
-        zz[z] = jnp.sum(xr[...], axis=0)
-        for k in range(1, NZ):
-            red_send(10 + k, zz.at[z], zz.at[z], z_peers[k - 1])
-
-    def red_x_back():
-        for k in range(1, NZ):
-            red_copy[10 + k].wait_recv()
-        rows = pl.ds(pl.multiple_of(y * 32 + x * 8, 8), 8)
-        wh[rows] = jnp.sum(zz[...], axis=0) * (1.0 / math.sqrt(SLABS * 8 * ROWS))
-        for k in range(1, NX):
-            red_send(17 + k, wh.at[rows], wh.at[rows], x_peers[k - 1])
+            red_send(14 + k, xr.at[x], xr.at[x], x_peers[k - 1])
 
     def red_y_back():
         for k in range(1, NX):
-            red_copy[17 + k].wait_recv()
+            red_copy[14 + k].wait_recv()
         rows = pl.ds(pl.multiple_of(y * 32, 32), 32)
+        wh[rows] = jnp.sum(xr[...], axis=0) * (1.0 / math.sqrt(SLABS * 8 * ROWS))
         for k in range(1, NY):
-            red_send(20 + k, wh.at[rows], wh.at[rows], y_peers[k - 1])
+            red_send(17 + k, wh.at[rows], wh.at[rows], y_peers[k - 1])
 
     def red_core_back():
         for k in range(1, NY):
-            red_copy[20 + k].wait_recv()
+            red_copy[17 + k].wait_recv()
         gwb[core] = wh[...]
-        red_send(28, gwb.at[core], gwb.at[core], partner)
+        red_send(25, gwb.at[core], gwb.at[core], partner)
 
     def spread_begin(d, c):
         for h in range(2):
-            rows = slice(h * HALF, (h + 1) * HALF)
-            high, low = split(g[d, h, c])
-            x_cat[c, rows, 0:HALF] = high
-            x_cat[c, rows, HALF:2 * HALF] = low
-
-    def spread_stop(d, c, s, first=False):
-        both = dot(t_hi[d, s], x_cat[c, 0:ROWS])
-        rest = dot(t_lo[d, s], x_cat[c, 0:ROWS, 0:HALF])
-        term = both[:, 0:HALF] + (both[:, HALF:2 * HALF] + rest)
-        sp[c, s] = term if first else sp[c, s] + term
+            put_parts(c, h * HALF, g[d, h, c], ROWS)
 
     def spread(own, x_at, c, first=False):
         d = place_of(own, x_at)
         spread_begin(d, c)
 
-        def one_stop(s, carry):
-            spread_stop(d, c, s, first)
-            return carry
-
-        lax.fori_loop(0, STOPS, one_stop, 0)
+        term = dot(t_cat[d], x_cat[c, 0:2 * ROWS])
+        acc[c] = term if first else acc[c] + term
+
+    def spread_stops(d, c, low, high):
+        rows = pl.ds(low * ROWS, (high - low) * ROWS)
+        total = acc[c, rows] + dot(t_cat[d, rows], x_cat[c, 0:2 * ROWS])
+        folded = total[:, 0:HALF] + total[:, HALF:2 * HALF]
+        for s in range(low, high):
+            sp[c, s] = folded[(s - low) * ROWS:(s - low + 1) * ROWS]
 
     def spread_sides(own, c):
         for k, x_at in ((1, x_right), (0, x_left)):
@@ -414,15 +406,10 @@
             return
         d = place_of(own, x_opp)
         spread_begin(d, c)
-        spread_stop(d, c, STOPS - 1)
+        spread_stops(d, c, STOPS - 1, STOPS)
         ring_send(c, 0, 0)
         ring_send(c, 0, 1)
-
-        def one_stop(i, carry):
-            spread_stop(d, c, STOPS - 2 - i)
-            return carry
-
-        lax.fori_loop(0, STOPS - 1, one_stop, 0)
+        spread_stops(d, c, 0, STOPS - 1)
 
     ring_copy = {}
 
@@ -447,40 +434,39 @@
             store(gf.at[c], gf_hbm.at[:, pl.ds(c * HALF, HALF)], 2 + c)
 
     ag_across(0, 0)
+    red_y()
     spread(1, x, 0, first=True)
     ag_relay(1, 1, 0)
     ag_relay(1, 1, 1)
-    red_y()
     spread(1, x, 1, first=True)
     ag_across(0, 1)
     spread_sides(1, 0)
+    red_z()
     ag_relay(0, 0, 0)
     spread_sides(1, 1)
     ag_across(1, 0)
     spread(0, x, 0)
     spread_opposite(1, 0)
     ag_relay(0, 0, 1)
-    red_x()
     spread_opposite(1, 1)
     ag_across(1, 1)
     ag_relay(0, 1, 0)
+    red_x()
     spread(0, x, 1)
     spread_sides(0, 0)
     ag_relay(0, 1, 1)
     spread_opposite(0, 0)
-    red_z()
+    red_y_back()
     spread_sides(0, 1)
     ring_step(0, 0)
     spread_opposite(0, 1)
-    red_x_back()
     ring_step(0, 1)
+    red_core_back()
     ring_step(1, 0)
-    red_y_back()
     ring_step(0, 2)
     ring_step(1, 1)
-    red_core_back()
     ring_step(1, 2)
-    red_copy[28].wait_recv()
+    red_copy[25].wait_recv()
     for c in range(2):
         store(gwb.at[c], gw_hbm.at[:, pl.ds(c * HALF, HALF)], 4 + c)
     for copy in stores:
@@ -490,17 +476,20 @@
 
 
 def write_out(act, gf, gw, act_out, gf_out, gw_out, held, sems):
-    for first, refs in ((0, (act, gf, gw)), (3, (act_out, gf_out, gw_out))):
-        copies = [
-            pltpu.make_async_copy(ref, held.at[i], sems.at[first + i])
-            if first == 0
-            else pltpu.make_async_copy(held.at[i], ref, sems.at[first + i])
-            for i, ref in enumerate(refs)
-        ]
-        for copy in copies:
-            copy.start()
-        for copy in copies:
-            copy.wait()
+    loads = [
+        pltpu.make_async_copy(ref, held.at[i], sems.at[i]) for i, ref in enumerate((act, gf, gw))
+    ]
+    stores = [
+        pltpu.make_async_copy(held.at[i], ref, sems.at[3 + i])
+        for i, ref in enumerate((act_out, gf_out, gw_out))
+    ]
+    for copy in loads:
+        copy.start()
+    for load, copy in zip(loads, stores):
+        load.wait()
+        copy.start()
+    for copy in stores:
+        copy.wait()
 
 
 def layer(pos, count, features, weight, cotangent, tiles):
@@ -520,12 +509,10 @@
         pltpu.VMEM((HID, HID), BF),
         pltpu.VMEM((ROWS, HID), F32),
         pltpu.VMEM((ROWS, HID), F32),
-        pltpu.VMEM((8, ROWS, STOPS * ROWS), BF),
-        pltpu.VMEM((8, ROWS, STOPS * ROWS), BF),
-        pltpu.VMEM((8, STOPS, ROWS, ROWS), BF),
-        pltpu.VMEM((8, STOPS, ROWS, ROWS), BF),
+        pltpu.VMEM((8, ROWS, 2 * BAND), BF),
+        pltpu.VMEM((8, BAND, 2 * ROWS), BF),
         pltpu.VMEM((STOPS, 2) + block, F32),
-        pltpu.VMEM((2, STOPS * ROWS, 2 * HALF), BF),
+        pltpu.VMEM((2, 2 * BAND, 2 * HALF), BF),
         pltpu.VMEM((4, 4, 2) + piece, F32),
         pltpu.VMEM((4, 2) + piece, F32),
         pltpu.VMEM((4, 2, 2) + piece, F32),
@@ -533,13 +520,14 @@
         pltpu.VMEM((2, 2) + piece, F32),
         pltpu.VMEM((ROWS, HID), F32),
         pltpu.VMEM((8, 2, 2) + piece, F32),
+        pltpu.VMEM((2, BAND, HID), F32),
         pltpu.VMEM((2, STOPS) + block, F32),
         pltpu.VMEM((STOPS - 1, 2) + block, F32),
         pltpu.VMEM((2,) + block, F32),
         pltpu.VMEM(block, F32),
         pltpu.VMEM((NY, 32, HALF), F32),
-        pltpu.VMEM((NX, 8, HALF), F32),
-        pltpu.VMEM((NZ, 8, HALF), F32),
+        pltpu.VMEM((NX, 32, HALF), F32),
+        pltpu.VMEM((NZ, 32, HALF), F32),
         pltpu.VMEM(block, F32),
         pltpu.VMEM((2,) + block, F32),
         dma(6), dma(6),
@@ -549,7 +537,7 @@
         dma(2, 2, 2, 3), dma(2, 2, 2, 3),
         dma(2, 2), dma(2, 2),
         dma(2, 3, 2), dma(2, 3, 2),
-        dma(29), dma(29),
+        dma(26), dma(26),
     ]
     outs = (
         jax.ShapeDtypeStruct((ROWS, HID), F32),

time: 91.2 us -> 87.9 us (0.964)
  Pallas kernels: 89.8 us -> 86.3 us
    pallas_call x1, Pallas kernels: 87.7 us -> 84.4 us  [layer(): pl.pallas_call(kernel, out_shape=outs, in_specs=[smem, smem, hbm, hbm, hb...]
where the time goes in v3:
time: 87.9 us; the launch traced here: 87.7 us
  Pallas kernels  86.3 us (98%)
  between operations  1.45 us (2%)
    pallas_call x1, Pallas kernels, layer(): pl.pallas_call(kernel, out_shape=outs, in_specs=[smem, smem, hbm, hbm, hb...  84.4 us
    pallas_call x1, Pallas kernels, layer(): pl.pallas_call(write_out, out_shape=outs, in_specs=[hbm, hbm, hbm], out_s...  1.88 us

profile of v3, /device:TPU:1, one launch (start us, length us, event | category | flops | bytes accessed | tf_op | source)
XLA Modules:
  0.0 87.7 jit_solution(1296833923054202511)
XLA Ops:
  1.3 84.4 %graph_layer.1 = (f32[256,256]{1,0:T(8,128)}, f32[256,256]{1,0:T(8,128)}, f32[256,256]{1,0:T(8,128)}) custom-call(s32[1,1,40]{2,1,0:T(1,128)} %pos.1, s32[1,1]{1,0:T(1,128)S(6)} %copy.9.count, f32[256,256]{1,0:T(8,128)} %feat.1, f32[256,256]{1,0:T(8,128)} %weight_hbm.1, f32[256,256]{1,0:T(8,128)} %cot_hbm.1, f32[1,1,40,128,128]{4,3,2,1,0:T(8,128)} %tiles_hbm.1), custom_call_target="tpu_custom_call" | custom-call | tf_op jit(solution)/shard_map/graph_layer/pallas_call | solution.py:547
  85.7 1.9 %write_out.1 = (f32[256,256]{1,0:T(8,128)}, f32[256,256]{1,0:T(8,128)}, f32[256,256]{1,0:T(8,128)}) custom-call(f32[256,256]{1,0:T(8,128)} %get-tuple-element.6.act, f32[256,256]{1,0:T(8,128)} %get-tuple-element.7.gf, f32[256,256]{1,0:T(8,128)} %get-tuple-element.8.gw), custom_call_target="tpu_custom_call" | custom-call | tf_op jit(solution)/shard_map/write_out/pallas_call | solution.py:558
